TPU v7x, 128 devices: a whole 4x4x4 slice. The times are simulated.
128 devices in a mesh: dp: 8 (over z, y_hi), tensor: 16 (over y_lo, x, core).
Axes of the slice: x: 4, y: 4 (y_hi: 2, y_lo: 2; y = y_hi * 2 + y_lo), z: 4, core: 2. Of those that a mesh axis runs over, the one named last changes fastest.
Arguments:
- hidden_act: bfloat16 [4096, 18432], P('dp', 'tensor'), may hold values from -0.09375 to 0.09375
- out_grad: bfloat16 [4096, 4608], P('dp', 'tensor'), may hold values from -6 to 6
- down_weight: bfloat16 [18432, 4608], P(None, 'tensor'), may hold values from -0.125 to 0.125
Outputs:
- hidden_grad: bfloat16 [18432, 4096], P('tensor', 'dp')
- weight_grad: float32 [18432, 4608], P(('tensor', 'dp'))
All inputs are finite; a program needn't handle non-finite values.
Results may differ from a plain program's by a relative error of at most 0.022.
Values may be sent and summed in bfloat16 or wider, within the bound.
A program may use at most 192 MiB of HBM per device.

v0:
```python
import jax
import jax.numpy as jnp
from jax import lax
from jax.sharding import PartitionSpec as P


def per_device(hidden_act, out_grad, down_weight):
    full_grad = lax.all_gather(out_grad, "tensor", axis=1, tiled=True)
    hidden_grad = lax.psum_scatter(
        lax.dot_general(
            down_weight, out_grad, (((1,), (1,)), ((), ())), preferred_element_type=jnp.float32
        ).astype(jnp.bfloat16),
        "tensor",
        scatter_dimension=0,
        tiled=True,
    )
    weight_grad = lax.psum_scatter(
        lax.dot_general(
            hidden_act, full_grad, (((0,), (0,)), ((), ())), preferred_element_type=jnp.float32
        ).astype(jnp.bfloat16),
        "dp",
        scatter_dimension=0,
        tiled=True,
    ).astype(jnp.float32)
    return (hidden_grad, weight_grad)


def solution(mesh):
    return jax.shard_map(
        per_device,
        mesh=mesh,
        in_specs=(P("dp", "tensor"), P("dp", "tensor"), P(None, "tensor")),
        out_specs=(P("tensor", "dp"), P(("tensor", "dp"), None)),
        check_vma=False,
    )
```

profile of v0, /device:TPU:9, one launch (start us, length us, event | category | flops | bytes accessed | tf_op | source)
XLA Modules:
  0.0 310.3 jit_solution(12735191657213053069)
XLA Ops:
  7.2 0.0 copy-start
  7.2 0.0 all-gather.2.cloned.1.call-start
  7.2 0.7 all-gather.2.cloned.1.call-update
  7.9 0.0 reduce-scatter.5.cloned.1.call-start
  8.0 42.4 %all-gather.2.cloned.1.call-done = bf16[512,4608]{0,1:T(8,128)(2,1)} async-done(((bf16[512,288]{0,1:T(8,128)(2,1)}), bf16[512,4608]{0,1:T(8,128)(2,1)}) %all-gather.2.cloned.1.call-update) | async-done | bytes 4718608 | tf_op jit(solution)/shard_map/all_gather | solution.py:8
  50.4 0.0 copy-done
  50.4 10.4 %convolution_convert_fusion.1 = bf16[1152,4608]{1,0:T(8,128)(2,1)} fusion(bf16[512,1152]{1,0:T(8,128)(2,1)S(1)} %copy-done, bf16[512,4608]{0,1:T(8,128)(2,1)} %all-gather.2.cloned.1.call-done), kind=kOutput, calls=%fused_computation.1 | convolution fusion | flops 5441126400 | bytes 16515072 | tf_op jit(solution)/shard_map/dot_general | solution.py:18
  60.8 0.0 copy-start.1
  60.8 0.0 reduce-scatter.5.cloned.1.call-update
  60.9 0.0 reduce-scatter.3.cloned.1.call-start
  60.9 0.9 copy-done.1
  61.8 18.0 %convolution_convert_fusion = bf16[18432,512]{1,0:T(8,128)(2,1)} fusion(bf16[18432,288]{0,1:T(8,128)(2,1)} %param.5, bf16[512,288]{0,1:T(8,128)(2,1)S(1)} %copy-done.1), kind=kOutput, calls=%fused_computation | convolution fusion | flops 5445255168 | bytes 29786112 | tf_op jit(solution)/shard_map/dot_general | solution.py:10
  79.8 0.0 reduce-scatter.3.cloned.1.call-update
  79.8 114.2 %reduce-scatter.5.cloned.1.call-done = bf16[144,4608]{1,0:T(8,128)(2,1)} async-done(((bf16[1152,4608]{1,0:T(8,128)(2,1)}), bf16[144,4608]{1,0:T(8,128)(2,1)}) %reduce-scatter.5.cloned.1.call-update) | async-done | bytes 1327120 | tf_op jit(solution)/shard_map/reduce_scatter | solution.py:17
  194.0 3.1 convert_element_type.11
  197.1 106.7 %reduce-scatter.3.cloned.1.call-done = bf16[1152,512]{1,0:T(8,128)(2,1)} async-done(((bf16[18432,512]{1,0:T(8,128)(2,1)}), bf16[1152,512]{1,0:T(8,128)(2,1)}) %reduce-scatter.3.cloned.1.call-update) | async-done | bytes 1179664 | tf_op jit(solution)/shard_map/reduce_scatter | solution.py:9
Async XLA Ops:
  7.2 43.2 %copy-start = (bf16[512,1152]{1,0:T(8,128)(2,1)S(1)}, bf16[512,1152]{1,0:T(8,128)(2,1)}, u32[]{:S(2)}) copy-start(bf16[512,1152]{1,0:T(8,128)(2,1)} %param.3) | copy-start | bytes 3538948
  7.2 43.2 %all-gather.2.cloned.1.call-start = ((), (), s32[]{:S(2)}) async-start(), calls=%async_computation.3 | async-start | bytes 5013504 | tf_op jit(solution)/shard_map/all_gather | solution.py:8
  7.9 186.1 %reduce-scatter.5.cloned.1.call-start = ((), (), s32[]{:S(2)}) async-start(), calls=%async_computation.4 | async-start | bytes 11943936 | tf_op jit(solution)/shard_map/reduce_scatter | solution.py:17
  60.8 1.0 copy-start.1
  60.9 243.0 %reduce-scatter.3.cloned.1.call-start = ((), (), s32[]{:S(2)}) async-start(), calls=%async_computation.2 | async-start | bytes 20054016 | tf_op jit(solution)/shard_map/reduce_scatter | solution.py:9
Sparse Core Ops, SparseCore 0:
  9.7 40.6 all-gather.1
  61.0 132.9 reduce-scatter.4
  197.1 106.6 reduce-scatter.2
where the time goes:
time: 312 us; the launch traced here: 310 us
  waiting for transfers between devices  264 us (85%)
  matrix products  28.4 us (9%)
  between operations  13.8 us (4%)
    reduce_scatter x1, waiting for transfers between devices, per_device(): lax.psum_scatter(lax.dot_general(hidden_act, full_grad, (((0,), (0,)), ((...  114 us
    reduce_scatter x1, waiting for transfers between devices, per_device(): lax.psum_scatter(lax.dot_general(down_weight, out_grad, (((1,), (1,)), ((...  107 us
    all_gather x1, waiting for transfers between devices, per_device(): full_grad = lax.all_gather(out_grad, 'tensor', axis=1, tiled=True)  42.4 us
    dot_general x1, matrix products, per_device(): lax.dot_general(down_weight, out_grad, (((1,), (1,)), ((), ())), preferre...  18 us
    dot_general x1, matrix products, per_device(): lax.dot_general(hidden_act, full_grad, (((0,), (0,)), ((), ())), preferre...  10.4 us
  transfers between devices with their start and end apart: 3, of which 3 were waited for; matrix products, arithmetic and copies ran while one was open for 7% of the time, Pallas kernels for 0%

commit v1 on v0

v1 whole, which is shorter than its diff:
```python
import functools

import jax
import jax.numpy as jnp
from jax import lax
from jax.experimental import pallas as pl
from jax.experimental.pallas import tpu as pltpu
from jax.sharding import PartitionSpec as P

MESH = pl.DeviceIdType.MESH
BF = jnp.bfloat16
F32 = jnp.float32
DB = 288
HB = 144
TB = 512
FB = 1152
ROW = 4 * DB
PARTS = ((0, 640), (640, 512))
TILE = 384

W_MOVES = [(1, 0, 0, DB), (-1, 0, 0, DB), (2, 0, 0, DB)]
for _dx in (0, 1, -1, 2):
    W_MOVES += [(_dx, 1, 0, HB), (_dx, -1, HB, HB)]
N_W = len(W_MOVES)
PARTNERS = [(1, 0, 0, 0), (-1, 0, 0, 0), (2, 0, 0, 0), (0, 2, 0, 0), (0, 0, 1, 0), (0, 0, -1, 0), (0, 0, 0, 1), (0, 2, 0, 1)]
PARTNERS += [(dx, dy, 0, 0) for dx in (0, 1, -1, 2) for dy in (1, -1)]
NT = (((1,), (1,)), ((), ()))


def kernel(a_ref, g_ref, w_ref, hg_ref, wg_ref, G, Wb, Wt, T, AT, SB, FW, RV, H, OWN, XS, XR, XB, YB, R, ss, rs, ws, wr, ls):
    t = lax.axis_index("tensor")
    r = lax.axis_index("dp")
    c = lax.rem(t, 2)
    x = lax.rem(t // 2, 4)
    l = t // 8
    h = lax.rem(r, 2)
    z = r // 2
    y = 2 * h + l

    def dev(dx, dy, dz, dc):
        X = lax.rem(x + (dx + 4), 4)
        Y = lax.rem(y + (dy + 4), 4)
        Z = lax.rem(z + (dz + 4), 4)
        C = lax.rem(c + dc, 2)
        return (Z * 2 + Y // 2, lax.rem(Y, 2) * 8 + X * 2 + C)

    def rcopy(k, src, dst, offset):
        return pltpu.make_async_remote_copy(
            src_ref=src, dst_ref=dst, send_sem=ss.at[k], recv_sem=rs.at[k], device_id=dev(*offset), device_id_type=MESH
        )

    started = []

    def go(k, src, dst, offset):
        cp = rcopy(k, src, dst, offset)
        cp.start()
        started.append(cp)
        return cp

    barrier = pltpu.get_barrier_semaphore()
    for offset in PARTNERS:
        pl.semaphore_signal(barrier, inc=1, device_id=dev(*offset), device_id_type=MESH)
    pl.semaphore_wait(barrier, len(PARTNERS))

    def slot(rep, ll, xx, lo=0, n=DB):
        return G.at[rep, pl.ds(pl.multiple_of((ll * 4 + xx) * DB + lo, 16), n), :]

    xm = lax.rem(x + 3, 4)
    xp = lax.rem(x + 1, 4)
    o = 1 - h
    k0 = go(0, g_ref, slot(h, l, x), (1, 0, 0, 0))
    k1 = go(1, g_ref, slot(h, l, x), (-1, 0, 0, 0))
    k2 = go(2, g_ref, slot(h, l, x), (0, 2, 0, 0))
    fo = pl.multiple_of((l * 8 + x * 2 + h) * FB, 128)
    own_w = pltpu.make_async_copy(
        w_ref.at[:, pl.ds(fo, FB)], Wb.at[pl.ds(pl.multiple_of((l * 4 + x) * DB, 16), DB), :], ls.at[0]
    )
    own_w.start()
    G[h, pl.ds(pl.multiple_of((l * 4 + x) * DB, 16), DB), :] = g_ref[...]

    T[...] = a_ref[...].T.reshape(4, 2, HB, TB)
    k11 = go(11, T.at[:, o], AT.at[h, :, c], (0, 2, 0, 0))
    AT[h, :, c] = T[:, h]
    k12 = go(12, AT.at[h, :, c], AT.at[h, :, c], (0, 0, 0, 1))

    k0.wait_recv()
    k3 = go(3, slot(h, l, xm, 0, HB), slot(h, l, xm, 0, HB), (1, 0, 0, 0))
    k1.wait_recv()
    k4 = go(4, slot(h, l, xp, HB, HB), slot(h, l, xp, HB, HB), (-1, 0, 0, 0))
    k2.wait_recv()
    k5 = go(5, slot(o, l, x), slot(o, l, x), (1, 0, 0, 0))
    k6 = go(6, slot(o, l, x), slot(o, l, x), (-1, 0, 0, 0))
    k3.wait_recv()
    k4.wait_recv()
    own_row = G.at[h, pl.ds(pl.multiple_of(l * ROW, 16), ROW), :]
    k7 = go(7, own_row, own_row, (0, 1, 0, 0))
    k8 = go(8, own_row, own_row, (0, -1, 0, 0))
    k5.wait_recv()
    k9 = go(9, slot(o, l, xm, 0, HB), slot(o, l, xm, 0, HB), (1, 0, 0, 0))
    k6.wait_recv()
    k10 = go(10, slot(o, l, xp, HB, HB), slot(o, l, xp, HB, HB), (-1, 0, 0, 0))

    w_copies = [[], []]

    def send_weights(p):
        lo, n = PARTS[p]
        for i, (dx, dy, first, rows) in enumerate(W_MOVES):
            X = lax.rem(x + (dx + 4), 4)
            Y = lax.rem(y + (dy + 4), 4)
            col = pl.multiple_of((lax.rem(Y, 2) * 8 + X * 2 + Y // 2) * FB + lo, 128)
            cp = pltpu.make_async_remote_copy(
                src_ref=w_ref.at[pl.ds(first, rows), pl.ds(col, n)],
                dst_ref=Wb.at[pl.ds(pl.multiple_of((l * 4 + x) * DB + first, 16), rows), pl.ds(lo, n)],
                send_sem=ws.at[p, i],
                recv_sem=wr.at[p, i],
                device_id=dev(dx, dy, 0, 0),
                device_id_type=MESH,
            )
            cp.start()
            w_copies[p].append(cp)

    send_weights(0)

    k11.wait_recv()
    k13 = go(13, AT.at[o, :, c], AT.at[o, :, c], (0, 0, 0, 1))
    k12.wait_recv()
    k13.wait_recv()
    k9.wait_recv()
    k10.wait_recv()

    def tile(zz, ll, n):
        rows = pl.ds(pl.multiple_of(ll * ROW + n * TILE, 16), TILE)
        acc = lax.dot_general(AT[0, zz].reshape(2 * HB, TB), G[0, rows, :], NT, preferred_element_type=F32)
        acc += lax.dot_general(AT[1, zz].reshape(2 * HB, TB), G[1, rows, :], NT, preferred_element_type=F32)
        return acc

    def cols(n):
        return pl.ds(pl.multiple_of(n * TILE, 128), TILE)

    zp = lax.rem(z + 1, 4)
    zm = lax.rem(z + 3, 4)
    zo = lax.rem(z + 2, 4)

    def chunk_send(j):
        ll = l if j == 0 else 1 - l
        base = 14 + 8 * j

        @pl.loop(0, ROW // TILE)
        def _(n):
            SB[j, 0, :, :, cols(n)] = tile(zo, ll, n).reshape(2, HB, TILE).astype(BF)

        up = go(base + 0, SB.at[j, 0, 0], FW.at[j, 0], (0, 0, 1, 0))
        down = go(base + 1, SB.at[j, 0, 1], FW.at[j, 1], (0, 0, -1, 0))

        @pl.loop(0, ROW // TILE)
        def _(n):
            part = tile(zp, ll, n).reshape(2, HB, TILE)
            SB[j, 1, 1, :, cols(n)] = part[1].astype(BF)
            H[0, :, cols(n)] = part[0]

        c0 = go(base + 2, SB.at[j, 1, 1], RV.at[j, 0, 1], (0, 0, 1, 0))

        @pl.loop(0, ROW // TILE)
        def _(n):
            part = tile(zm, ll, n).reshape(2, HB, TILE)
            SB[j, 2, 0, :, cols(n)] = part[0].astype(BF)
            H[1, :, cols(n)] = part[1]

        c1 = go(base + 3, SB.at[j, 2, 0], RV.at[j, 1, 0], (0, 0, -1, 0))
        up.wait_recv()
        SB[j, 1, 0] = (H[0] + FW[j, 0].astype(F32)).astype(BF)
        c2 = go(base + 4, SB.at[j, 1, 0], RV.at[j, 0, 0], (0, 0, 1, 0))
        down.wait_recv()
        SB[j, 2, 1] = (H[1] + FW[j, 1].astype(F32)).astype(BF)
        c3 = go(base + 5, SB.at[j, 2, 1], RV.at[j, 1, 1], (0, 0, -1, 0))
        return c0, c1, c2, c3

    def chunk_own(j):
        ll = l if j == 0 else 1 - l

        @pl.loop(0, ROW // TILE)
        def _(n):
            OWN[j, :, :, cols(n)] = tile(z, ll, n).reshape(2, HB, TILE)

    def chunk_end(j, copies):
        for cp in copies:
            cp.wait_recv()
        XS[j] = (OWN[j, 1 - c] + RV[j, 0, 1 - c].astype(F32) + RV[j, 1, 1 - c].astype(F32)).astype(BF)
        swap = go(20 + 8 * j, XS.at[j], XR.at[j], (0, 0, 0, 1))
        OWN[j, c] = OWN[j, c] + RV[j, 0, c].astype(F32) + RV[j, 1, c].astype(F32)
        return swap

    def chunk_out(j, swap):
        ll = l if j == 0 else 1 - l
        swap.wait_recv()
        mine = OWN[j, c]
        other = XR[j].astype(F32)
        even = jnp.where(c == 0, mine, other)
        odd = jnp.where(c == 0, other, mine)
        pieces = []
        for xx in range(4):
            pieces += [even[:, xx * DB:(xx + 1) * DB], odd[:, xx * DB:(xx + 1) * DB]]
        wg_ref[:, pl.ds(pl.multiple_of(ll * 2 * ROW, 128), 2 * ROW)] = jnp.concatenate(pieces, axis=1)

    def hidden(p):
        lo, n = PARTS[p]
        if p == 0:
            own_w.wait()
        for cp in w_copies[p]:
            cp.wait_recv()

        @pl.loop(0, 2 * ROW // 256)
        def _(k):
            rows = pl.ds(pl.multiple_of(k * 256, 256), 256)
            Wt[pl.ds(0, n), rows] = Wb[rows, pl.ds(lo, n)].T

        def product(rep, q):
            return jnp.dot(Wt[pl.ds(0, n), :], G[rep, :, pl.ds(pl.multiple_of(q * 256, 256), 256)], preferred_element_type=F32)

        @pl.loop(0, 2)
        def _(q):
            XB[p, pl.ds(0, n), pl.ds(pl.multiple_of(q * 256, 256), 256)] = product(1 - c, q).astype(BF)

        half = rcopy(30 + 2 * p, XB.at[p, pl.ds(0, n)], YB.at[p, pl.ds(0, n)], (0, 0, 0, 1))
        half.start()

        @pl.loop(0, 2)
        def _(q):
            H2 = pl.ds(pl.multiple_of(q * 256, 256), 256)
            R[p, pl.ds(0, n), H2] = product(c, q)

        half.wait_recv()
        XB2 = (R[p, pl.ds(0, n), :] + YB[p, pl.ds(0, n), :].astype(F32)).astype(BF)
        half.wait_send()
        XB[p, pl.ds(0, n), :] = XB2
        final = rcopy(31 + 2 * p, XB.at[p, pl.ds(0, n)], hg_ref.at[pl.ds(lo, n)], (0, 2, 0, 1))

        @pl.when(c != h)
        def _():
            final.start()

        @pl.when(c == h)
        def _():
            hg_ref[pl.ds(lo, n), :] = XB2

        return final

    first = chunk_send(0)
    chunk_own(0)
    k7.wait_recv()
    k8.wait_recv()
    send_weights(1)
    second = chunk_send(1)
    chunk_own(1)
    swap0 = chunk_end(0, first)
    f0 = hidden(0)
    chunk_out(0, swap0)
    swap1 = chunk_end(1, second)
    f1 = hidden(1)
    chunk_out(1, swap1)

    @pl.when(c != h)
    def _():
        f0.wait()
        f1.wait()

    for cp in started:
        cp.wait_send()
    for p in range(2):
        for cp in w_copies[p]:
            cp.wait_send()


def per_device(hidden_act, out_grad, down_weight):
    scratch = [
        pltpu.VMEM((2, 2 * ROW, TB), BF),
        pltpu.VMEM((2 * ROW, FB), BF),
        pltpu.VMEM((640, 2 * ROW), BF),
        pltpu.VMEM((4, 2, HB, TB), BF),
        pltpu.VMEM((2, 4, 2, HB, TB), BF),
        pltpu.VMEM((2, 3, 2, HB, ROW), BF),
        pltpu.VMEM((2, 2, HB, ROW), BF),
        pltpu.VMEM((2, 2, 2, HB, ROW), BF),
        pltpu.VMEM((2, HB, ROW), F32),
        pltpu.VMEM((2, 2, HB, ROW), F32),
        pltpu.VMEM((2, HB, ROW), BF),
        pltpu.VMEM((2, HB, ROW), BF),
        pltpu.VMEM((2, 640, TB), BF),
        pltpu.VMEM((2, 640, TB), BF),
        pltpu.VMEM((2, 640, TB), F32),
        pltpu.SemaphoreType.DMA((34,)),
        pltpu.SemaphoreType.DMA((34,)),
        pltpu.SemaphoreType.DMA((2, N_W)),
        pltpu.SemaphoreType.DMA((2, N_W)),
        pltpu.SemaphoreType.DMA((1,)),
    ]
    vmem = pl.BlockSpec(memory_space=pltpu.VMEM)
    return pl.pallas_call(
        kernel,
        out_shape=(jax.ShapeDtypeStruct((FB, TB), BF), jax.ShapeDtypeStruct((HB, 16 * DB), F32)),
        in_specs=[vmem, vmem, pl.BlockSpec(memory_space=pl.ANY)],
        out_specs=(vmem, vmem),
        scratch_shapes=scratch,
        compiler_params=pltpu.CompilerParams(collective_id=0, has_side_effects=True, vmem_limit_bytes=60 * 2**20),
        cost_estimate=pl.CostEstimate(flops=10_900_000_000, bytes_accessed=20_000_000, transcendentals=0),
    )(hidden_act, out_grad.T, down_weight.T)


def solution(mesh):
    return jax.shard_map(
        per_device,
        mesh=mesh,
        in_specs=(P("dp", "tensor"), P("dp", "tensor"), P(None, "tensor")),
        out_specs=(P("tensor", "dp"), P(("tensor", "dp"), None)),
        check_vma=False,
    )
```

time: 312 us -> 120 us (0.38)
  waiting for transfers between devices: 264 us -> 0 us
  Pallas kernels: 0 us -> 114 us
  matrix products: 28.4 us -> 0 us
  between operations: 13.8 us -> 0.64 us
  local copies, waits for them, and re-layouts: 0.9 us -> 5.78 us
    reduce_scatter x2 -> x0, waiting for transfers between devices: 221 us -> none  [the longest x1 114 us: per_device(): lax.psum_scatter(lax.dot_general(hidden_act, full_grad, (((0,), (0,)), ((...]
    pallas_call x0 -> x1, Pallas kernels: none -> 114 us  [per_device(): pl.pallas_call(kernel, out_shape=(jax.ShapeDtypeStruct((FB, TB), BF), jax...]
    all_gather x1 -> x0, waiting for transfers between devices: 42.4 us -> none  [per_device(): full_grad = lax.all_gather(out_grad, 'tensor', axis=1, tiled=True)]
    dot_general x2 -> x0, matrix products: 28.4 us -> none  [the longest x1 18 us: per_device(): lax.dot_general(down_weight, out_grad, (((1,), (1,)), ((), ())), preferre...]
    unnamed x4 -> x2, local copies, waits for them, and re-layouts: 0.9 us -> 5.78 us
  transfers between devices with their start and end apart: 3 -> 0, of which waited for: 3 -> 0; matrix products, arithmetic and copies ran while one was open for 7% -> 0% of each run, Pallas kernels for 0% -> 0%
where the time goes in v1:
time: 120 us
  Pallas kernels  114 us (95%)
  local copies, waits for them, and re-layouts  5.78 us (5%)
    pallas_call x1, Pallas kernels, per_device(): pl.pallas_call(kernel, out_shape=(jax.ShapeDtypeStruct((FB, TB), BF), jax...  114 us
    unnamed x2, local copies, waits for them, and re-layouts  5.78 us

profile of v1, /device:TPU:9, one launch (start us, length us, event | category | flops | bytes accessed | tf_op | source)
XLA Modules:
  0.0 120.0 jit_solution(17831202039727420352)
XLA Ops:
  0.6 113.6 %shard_map.50 = (bf16[1152,512]{1,0:T(8,128)(2,1)}, f32[144,4608]{1,0:T(8,128)}) custom-call(bf16[512,1152]{1,0:T(8,128)(2,1)} %a_ref.1, bf16[288,512]{1,0:T(8,128)(2,1)} %bitcast.3, bf16[288,18432]{1,0:T(8,128)(2,1)} %bitcast.2), custom_call_target="tpu_custom_call" | custom-call | flops 10899999744 | bytes 20000000 | tf_op jit(solution)/shard_map/pallas_call | solution.py:298
  114.2 2.4 %copy.7 = bf16[1152,512]{1,0:T(8,128)(2,1)} copy(bf16[1152,512]{1,0:T(8,128)(2,1)} %get-tuple-element.4) | data formatting | bytes 2359296
  116.6 3.4 %copy.8 = f32[144,4608]{1,0:T(8,128)} copy(f32[144,4608]{1,0:T(8,128)} %get-tuple-element.5) | data formatting | bytes 5308416

commit v2 on v1

--- a/solution.py
+++ b/solution.py
@@ -27,7 +27,7 @@
 NT = (((1,), (1,)), ((), ()))
 
 
-def kernel(a_ref, g_ref, w_ref, hg_ref, wg_ref, G, Wb, Wt, T, AT, SB, FW, RV, H, OWN, XS, XR, XB, YB, R, ss, rs, ws, wr, ls):
+def kernel(a_hbm, g_hbm, w_ref, hg_ref, wg_ref, a_ref, g_ref, G, Wb, Wt, T, AT, SB, FW, RV, H, OWN, XS, XR, XB, YB, R, ss, rs, ws, wr, ls):
     t = lax.axis_index("tensor")
     r = lax.axis_index("dp")
     c = lax.rem(t, 2)
@@ -57,11 +57,16 @@
         started.append(cp)
         return cp
 
+    load_g = pltpu.make_async_copy(g_hbm, g_ref, ls.at[1])
+    load_g.start()
+    load_a = pltpu.make_async_copy(a_hbm, a_ref, ls.at[2])
+    load_a.start()
     barrier = pltpu.get_barrier_semaphore()
     for offset in PARTNERS:
         pl.semaphore_signal(barrier, inc=1, device_id=dev(*offset), device_id_type=MESH)
     pl.semaphore_wait(barrier, len(PARTNERS))
 
+    load_g.wait()
     def slot(rep, ll, xx, lo=0, n=DB):
         return G.at[rep, pl.ds(pl.multiple_of((ll * 4 + xx) * DB + lo, 16), n), :]
 
@@ -78,6 +83,7 @@
     own_w.start()
     G[h, pl.ds(pl.multiple_of((l * 4 + x) * DB, 16), DB), :] = g_ref[...]
 
+    load_a.wait()
     T[...] = a_ref[...].T.reshape(4, 2, HB, TB)
     k11 = go(11, T.at[:, o], AT.at[h, :, c], (0, 2, 0, 0))
     AT[h, :, c] = T[:, h]
@@ -273,6 +279,8 @@
 
 def per_device(hidden_act, out_grad, down_weight):
     scratch = [
+        pltpu.VMEM((TB, FB), BF),
+        pltpu.VMEM((DB, TB), BF),
         pltpu.VMEM((2, 2 * ROW, TB), BF),
         pltpu.VMEM((2 * ROW, FB), BF),
         pltpu.VMEM((640, 2 * ROW), BF),
@@ -292,18 +300,19 @@
         pltpu.SemaphoreType.DMA((34,)),
         pltpu.SemaphoreType.DMA((2, N_W)),
         pltpu.SemaphoreType.DMA((2, N_W)),
-        pltpu.SemaphoreType.DMA((1,)),
+        pltpu.SemaphoreType.DMA((3,)),
     ]
     vmem = pl.BlockSpec(memory_space=pltpu.VMEM)
-    return pl.pallas_call(
+    held = pl.pallas_call(
         kernel,
-        out_shape=(jax.ShapeDtypeStruct((FB, TB), BF), jax.ShapeDtypeStruct((HB, 16 * DB), F32)),
-        in_specs=[vmem, vmem, pl.BlockSpec(memory_space=pl.ANY)],
+        out_shape=(pltpu.VMEM((FB, TB), BF), pltpu.VMEM((HB, 16 * DB), F32)),
+        in_specs=[pl.BlockSpec(memory_space=pl.ANY)] * 3,
         out_specs=(vmem, vmem),
         scratch_shapes=scratch,
-        compiler_params=pltpu.CompilerParams(collective_id=0, has_side_effects=True, vmem_limit_bytes=60 * 2**20),
+        compiler_params=pltpu.CompilerParams(collective_id=0, has_side_effects=True, vmem_limit_bytes=63_000_000),
         cost_estimate=pl.CostEstimate(flops=10_900_000_000, bytes_accessed=20_000_000, transcendentals=0),
     )(hidden_act, out_grad.T, down_weight.T)
+    return held
 
 
 def solution(mesh):

time: 120 us -> 114 us (0.950)
  local copies, waits for them, and re-layouts: 5.78 us -> 2.52 us
  Pallas kernels: 114 us -> 111 us
    unnamed x2, local copies, waits for them, and re-layouts: 5.78 us -> 2.52 us
    pallas_call x1, Pallas kernels: 114 us -> 111 us  [per_device(): pl.pallas_call(kernel, out_shape=(pltpu.VMEM((FB, TB), BF), pltpu.VMEM((H...]
where the time goes in v2:
time: 114 us
  Pallas kernels  111 us (97%)
  local copies, waits for them, and re-layouts  2.52 us (2%)
    pallas_call x1, Pallas kernels, per_device(): pl.pallas_call(kernel, out_shape=(pltpu.VMEM((FB, TB), BF), pltpu.VMEM((H...  111 us
    unnamed x2, local copies, waits for them, and re-layouts  2.52 us

profile of v2, /device:TPU:9, one launch (start us, length us, event | category | flops | bytes accessed | tf_op | source)
XLA Modules:
  0.0 113.8 jit_solution(8185993363042311610)
XLA Ops:
  0.6 110.7 %shard_map.50 = (bf16[1152,512]{1,0:T(8,128)(2,1)S(1)}, f32[144,4608]{1,0:T(8,128)S(1)}) custom-call(bf16[512,1152]{1,0:T(8,128)(2,1)} %a_hbm.1, bf16[288,512]{1,0:T(8,128)(2,1)} %bitcast.3, bf16[288,18432]{1,0:T(8,128)(2,1)} %bitcast.2), custom_call_target="tpu_custom_call" | custom-call | flops 10899999744 | bytes 20000000 | tf_op jit(solution)/shard_map/pallas_call | solution.py:306
  111.3 1.0 copy.7
  112.3 1.5 %copy.8 = f32[144,4608]{1,0:T(8,128)} copy(f32[144,4608]{1,0:T(8,128)S(1)} %get-tuple-element.3) | data formatting | bytes 5308416

commit v3 on v2

v3 whole, which is shorter than its diff:
```python
import functools

import jax
import jax.numpy as jnp
from jax import lax
from jax.experimental import pallas as pl
from jax.experimental.pallas import tpu as pltpu
from jax.sharding import PartitionSpec as P

MESH = pl.DeviceIdType.MESH
BF = jnp.bfloat16
F32 = jnp.float32
DB = 288
HB = 144
TB = 512
FB = 1152
ROW = 4 * DB
PART = 384
N_PARTS = FB // PART
TILE = 384

NEAR = [(1, 0, 0, DB), (-1, 0, 0, DB), (2, 0, 0, DB)]
FAR = []
for _dx in (0, 1, -1, 2):
    FAR += [(_dx, 1, 0, HB), (_dx, -1, HB, HB)]
N_SEM = 80
PARTNERS = [(1, 0, 0, 0), (-1, 0, 0, 0), (2, 0, 0, 0), (0, 2, 0, 0), (0, 0, 1, 0), (0, 0, -1, 0), (0, 0, 0, 1), (0, 2, 0, 1)]
PARTNERS += [(dx, dy, 0, 0) for dx in (0, 1, -1, 2) for dy in (1, -1)]
NT = (((1,), (1,)), ((), ()))


def kernel(a_hbm, g_hbm, w_ref, hg_ref, wg_ref, a_ref, g_ref, G, Wb, Wt, T, AT, SB, FW, RV, H, OWN, XS, XR, XB, YB, XF, R, ss, rs, ls):
    t = lax.axis_index("tensor")
    r = lax.axis_index("dp")
    c = lax.rem(t, 2)
    x = lax.rem(t // 2, 4)
    l = t // 8
    h = lax.rem(r, 2)
    z = r // 2
    y = 2 * h + l

    def dev(dx, dy, dz, dc):
        X = lax.rem(x + (dx + 4), 4)
        Y = lax.rem(y + (dy + 4), 4)
        Z = lax.rem(z + (dz + 4), 4)
        C = lax.rem(c + dc, 2)
        return (Z * 2 + Y // 2, lax.rem(Y, 2) * 8 + X * 2 + C)

    count = [0]
    started = []

    def prepare(src, dst, offset):
        k = count[0]
        count[0] += 1
        return pltpu.make_async_remote_copy(
            src_ref=src, dst_ref=dst, send_sem=ss.at[k], recv_sem=rs.at[k], device_id=dev(*offset), device_id_type=MESH
        )

    def go(src, dst, offset):
        cp = prepare(src, dst, offset)
        cp.start()
        started.append(cp)
        return cp

    def same(ref, offset):
        return go(ref, ref, offset)

    load_g = pltpu.make_async_copy(g_hbm, g_ref, ls.at[1])
    load_g.start()
    load_a = pltpu.make_async_copy(a_hbm, a_ref, ls.at[2])
    load_a.start()
    barrier = pltpu.get_barrier_semaphore()
    for offset in PARTNERS:
        pl.semaphore_signal(barrier, inc=1, device_id=dev(*offset), device_id_type=MESH)
    pl.semaphore_wait(barrier, len(PARTNERS))

    load_g.wait()

    def slot(rep, xx, lo=0, n=DB):
        return G.at[rep, pl.ds(pl.multiple_of((l * 4 + xx) * DB + lo, 16), n), :]

    xm = lax.rem(x + 3, 4)
    xp = lax.rem(x + 1, 4)
    o = 1 - h
    RIGHT, LEFT, ACROSS, OTHER = (1, 0, 0, 0), (-1, 0, 0, 0), (0, 2, 0, 0), (0, 0, 0, 1)

    def own(lo, offset):
        return go(g_ref.at[pl.ds(lo, HB)], slot(h, x, lo, HB), offset)

    r0, l1, a0, a1, r1, l0 = own(0, RIGHT), own(HB, LEFT), own(0, ACROSS), own(HB, ACROSS), own(HB, RIGHT), own(0, LEFT)
    fo = pl.multiple_of((l * 8 + x * 2 + h) * FB, 128)
    own_w = pltpu.make_async_copy(
        w_ref.at[:, pl.ds(fo, FB)], Wb.at[pl.ds(pl.multiple_of((l * 4 + x) * DB, 16), DB), :], ls.at[0]
    )
    own_w.start()
    G[h, pl.ds(pl.multiple_of((l * 4 + x) * DB, 16), DB), :] = g_ref[...]

    load_a.wait()
    T[...] = a_ref[...].T.reshape(4, 2, HB, TB)
    act = go(T.at[:, o], AT.at[h, :, c], ACROSS)
    AT[h, :, c] = T[:, h]
    act_own = same(AT.at[h, :, c], OTHER)

    r0.wait_recv()
    r2 = same(slot(h, xm, 0, HB), RIGHT)
    l1.wait_recv()
    l2 = same(slot(h, xp, HB, HB), LEFT)
    a0.wait_recv()
    ar0 = same(slot(o, x, 0, HB), RIGHT)
    a1.wait_recv()
    al1 = same(slot(o, x, HB, HB), LEFT)
    ar1 = same(slot(o, x, HB, HB), RIGHT)
    al0 = same(slot(o, x, 0, HB), LEFT)
    for cp in (r1, l0, r2, l2):
        cp.wait_recv()
    own_row = G.at[h, pl.ds(pl.multiple_of(l * ROW, 16), ROW), :]
    row_up = same(own_row, (0, 1, 0, 0))
    row_down = same(own_row, (0, -1, 0, 0))
    ar0.wait_recv()
    ar2 = same(slot(o, xm, 0, HB), RIGHT)
    al1.wait_recv()
    al2 = same(slot(o, xp, HB, HB), LEFT)

    def units(p):
        return pl.ds(p * PART, PART)

    def send_weights(p, moves):
        copies = []
        for dx, dy, first, rows in moves:
            X = lax.rem(x + (dx + 4), 4)
            Y = lax.rem(y + (dy + 4), 4)
            col = pl.multiple_of((lax.rem(Y, 2) * 8 + X * 2 + Y // 2) * FB + p * PART, 128)
            there = pl.ds(pl.multiple_of((l * 4 + x) * DB + first, 16), rows)
            copies.append(go(w_ref.at[pl.ds(first, rows), pl.ds(col, PART)], Wb.at[there, units(p)], (dx, dy, 0, 0)))
        return copies

    near = [send_weights(p, NEAR) for p in range(N_PARTS)]
    far = [send_weights(p, FAR) for p in (0, 1, 2)]

    act.wait_recv()
    act_other = same(AT.at[o, :, c], OTHER)
    act_own.wait_recv()
    act_other.wait_recv()
    for cp in (ar1, al0, ar2, al2):
        cp.wait_recv()

    def tile(zz, ll, n):
        rows = pl.ds(pl.multiple_of(ll * ROW + n * TILE, 16), TILE)
        acc = lax.dot_general(AT[0, zz].reshape(2 * HB, TB), G[0, rows, :], NT, preferred_element_type=F32)
        acc += lax.dot_general(AT[1, zz].reshape(2 * HB, TB), G[1, rows, :], NT, preferred_element_type=F32)
        return acc

    def cols(n):
        return pl.ds(pl.multiple_of(n * TILE, 128), TILE)

    UP, DOWN = (0, 0, 1, 0), (0, 0, -1, 0)
    zp = lax.rem(z + 1, 4)
    zm = lax.rem(z + 3, 4)
    zo = lax.rem(z + 2, 4)

    def chunk_parts(j):
        ll = l if j == 0 else 1 - l

        @pl.loop(0, ROW // TILE)
        def _(n):
            SB[j, 0, :, :, cols(n)] = tile(zo, ll, n).reshape(2, HB, TILE).astype(BF)

        up = go(SB.at[j, 0, 0], FW.at[j, 0], UP)
        down = go(SB.at[j, 0, 1], FW.at[j, 1], DOWN)

        @pl.loop(0, ROW // TILE)
        def _(n):
            part = tile(zp, ll, n).reshape(2, HB, TILE)
            SB[j, 1, 1, :, cols(n)] = part[1].astype(BF)
            H[j, 0, :, cols(n)] = part[0]

        c0 = go(SB.at[j, 1, 1], RV.at[j, 0, 1], UP)

        @pl.loop(0, ROW // TILE)
        def _(n):
            part = tile(zm, ll, n).reshape(2, HB, TILE)
            SB[j, 2, 0, :, cols(n)] = part[0].astype(BF)
            H[j, 1, :, cols(n)] = part[1]

        c1 = go(SB.at[j, 2, 0], RV.at[j, 1, 0], DOWN)
        return up, down, c0, c1

    def chunk_sums(j, copies):
        up, down, c0, c1 = copies
        up.wait_recv()
        SB[j, 1, 0] = (H[j, 0] + FW[j, 0].astype(F32)).astype(BF)
        c2 = go(SB.at[j, 1, 0], RV.at[j, 0, 0], UP)
        down.wait_recv()
        SB[j, 2, 1] = (H[j, 1] + FW[j, 1].astype(F32)).astype(BF)
        c3 = go(SB.at[j, 2, 1], RV.at[j, 1, 1], DOWN)
        return c0, c1, c2, c3

    def chunk_own(j):
        ll = l if j == 0 else 1 - l

        @pl.loop(0, ROW // TILE)
        def _(n):
            OWN[j, :, :, cols(n)] = tile(z, ll, n).reshape(2, HB, TILE)

    def chunk_end(j, copies):
        for cp in copies:
            cp.wait_recv()
        XS[j] = (OWN[j, 1 - c] + RV[j, 0, 1 - c].astype(F32) + RV[j, 1, 1 - c].astype(F32)).astype(BF)
        swap = go(XS.at[j], XR.at[j], OTHER)
        OWN[j, c] = OWN[j, c] + RV[j, 0, c].astype(F32) + RV[j, 1, c].astype(F32)
        return swap

    def chunk_out(j, swap):
        ll = l if j == 0 else 1 - l
        swap.wait_recv()
        mine = OWN[j, c]
        other = XR[j].astype(F32)
        even = jnp.where(c == 0, mine, other)
        odd = jnp.where(c == 0, other, mine)
        pieces = []
        for xx in range(4):
            pieces += [even[:, xx * DB:(xx + 1) * DB], odd[:, xx * DB:(xx + 1) * DB]]
        wg_ref[:, pl.ds(pl.multiple_of(ll * 2 * ROW, 128), 2 * ROW)] = jnp.concatenate(pieces, axis=1)

    def half_tokens(q):
        return pl.ds(pl.multiple_of(q * 256, 256), 256)

    def product(rep, ll, q):
        g = G[rep, pl.ds(pl.multiple_of(ll * ROW, 16), ROW), half_tokens(q)]
        return jnp.dot(Wt[...], g, preferred_element_type=F32)

    def turn(p, ll):
        @pl.loop(0, ROW // 384)
        def _(k):
            rows = pl.ds(pl.multiple_of(ll * ROW + k * 384, 16), 384)
            Wt[:, pl.ds(pl.multiple_of(k * 384, 128), 384)] = Wb[rows, units(p)].T

    def hidden_near(p):
        for cp in near[p]:
            cp.wait_recv()
        turn(p, l)

        @pl.loop(0, 2)
        def _(q):
            R[p, 0, :, half_tokens(q)] = product(0, l, q)
            R[p, 1, :, half_tokens(q)] = product(1, l, q)

    def hidden_far(p):
        for cp in far[p]:
            cp.wait_recv()
        ll = 1 - l
        turn(p, ll)

        @pl.loop(0, 2)
        def _(q):
            XB[p, :, half_tokens(q)] = (R[p, 1 - c, :, half_tokens(q)] + product(1 - c, ll, q)).astype(BF)

        half = go(XB.at[p], YB.at[p], OTHER)

        @pl.loop(0, 2)
        def _(q):
            R[p, c, :, half_tokens(q)] += product(c, ll, q)

        half.wait_recv()
        XF[p] = (R[p, c] + YB[p].astype(F32)).astype(BF)
        final = prepare(XF.at[p], hg_ref.at[pl.ds(p * PART, PART)], (0, 2, 0, 1))

        @pl.when(c != h)
        def _():
            final.start()

        @pl.when(c == h)
        def _():
            hg_ref[pl.ds(p * PART, PART), :] = XF[p]

        return final

    first = chunk_parts(0)
    chunk_own(0)
    first = chunk_sums(0, first)
    row_up.wait_recv()
    row_down.wait_recv()
    second = chunk_parts(1)
    chunk_own(1)
    own_w.wait()
    hidden_near(0)
    second = chunk_sums(1, second)
    hidden_near(1)
    hidden_near(2)
    swap0 = chunk_end(0, first)
    chunk_out(0, swap0)
    f0 = hidden_far(0)
    f1 = hidden_far(1)
    f2 = hidden_far(2)
    swap1 = chunk_end(1, second)
    chunk_out(1, swap1)

    @pl.when(c != h)
    def _():
        for cp in (f0, f1, f2):
            cp.wait()

    for cp in started:
        cp.wait_send()


def per_device(hidden_act, out_grad, down_weight):
    scratch = [
        pltpu.VMEM((TB, FB), BF),
        pltpu.VMEM((DB, TB), BF),
        pltpu.VMEM((2, 2 * ROW, TB), BF),
        pltpu.VMEM((2 * ROW, FB), BF),
        pltpu.VMEM((PART, ROW), BF),
        pltpu.VMEM((4, 2, HB, TB), BF),
        pltpu.VMEM((2, 4, 2, HB, TB), BF),
        pltpu.VMEM((2, 3, 2, HB, ROW), BF),
        pltpu.VMEM((2, 2, HB, ROW), BF),
        pltpu.VMEM((2, 2, 2, HB, ROW), BF),
        pltpu.VMEM((2, 2, HB, ROW), F32),
        pltpu.VMEM((2, 2, HB, ROW), F32),
        pltpu.VMEM((2, HB, ROW), BF),
        pltpu.VMEM((2, HB, ROW), BF),
        pltpu.VMEM((N_PARTS, PART, TB), BF),
        pltpu.VMEM((N_PARTS, PART, TB), BF),
        pltpu.VMEM((N_PARTS, PART, TB), BF),
        pltpu.VMEM((N_PARTS, 2, PART, TB), F32),
        pltpu.SemaphoreType.DMA((N_SEM,)),
        pltpu.SemaphoreType.DMA((N_SEM,)),
        pltpu.SemaphoreType.DMA((3,)),
    ]
    vmem = pl.BlockSpec(memory_space=pltpu.VMEM)
    held = pl.pallas_call(
        kernel,
        out_shape=(pltpu.VMEM((FB, TB), BF), pltpu.VMEM((HB, 16 * DB), F32)),
        in_specs=[pl.BlockSpec(memory_space=pl.ANY)] * 3,
        out_specs=(vmem, vmem),
        scratch_shapes=scratch,
        compiler_params=pltpu.CompilerParams(collective_id=0, has_side_effects=True, vmem_limit_bytes=63_000_000),
        cost_estimate=pl.CostEstimate(flops=10_900_000_000, bytes_accessed=20_000_000, transcendentals=0),
    )(hidden_act, out_grad.T, down_weight.T)
    return held


def solution(mesh):
    return jax.shard_map(
        per_device,
        mesh=mesh,
        in_specs=(P("dp", "tensor"), P("dp", "tensor"), P(None, "tensor")),
        out_specs=(P("tensor", "dp"), P(("tensor", "dp"), None)),
        check_vma=False,
    )
```

time: 114 us -> 101 us (0.89)
  Pallas kernels: 111 us -> 97.7 us
    pallas_call x1, Pallas kernels: 111 us -> 97.7 us  [per_device(): pl.pallas_call(kernel, out_shape=(pltpu.VMEM((FB, TB), BF), pltpu.VMEM((H...]
where the time goes in v3:
time: 101 us
  Pallas kernels  97.7 us (97%)
  local copies, waits for them, and re-layouts  2.52 us (2%)
    pallas_call x1, Pallas kernels, per_device(): pl.pallas_call(kernel, out_shape=(pltpu.VMEM((FB, TB), BF), pltpu.VMEM((H...  97.7 us
    unnamed x2, local copies, waits for them, and re-layouts  2.52 us

profile of v3, /device:TPU:9, one launch (start us, length us, event | category | flops | bytes accessed | tf_op | source)
XLA Modules:
  0.0 100.8 jit_solution(6049723227851529972)
XLA Ops:
  0.6 97.7 %shard_map.50 = (bf16[1152,512]{1,0:T(8,128)(2,1)S(1)}, f32[144,4608]{1,0:T(8,128)S(1)}) custom-call(bf16[512,1152]{1,0:T(8,128)(2,1)} %a_hbm.1, bf16[288,512]{1,0:T(8,128)(2,1)} %bitcast.3, bf16[288,18432]{1,0:T(8,128)(2,1)} %bitcast.2), custom_call_target="tpu_custom_call" | custom-call | flops 10899999744 | bytes 20000000 | tf_op jit(solution)/shard_map/pallas_call | solution.py:332
  98.3 1.0 %copy.7 = bf16[1152,512]{1,0:T(8,128)(2,1)} copy(bf16[1152,512]{1,0:T(8,128)(2,1)S(1)} %get-tuple-element.2) | data formatting | bytes 2359296
  99.3 1.5 %copy.8 = f32[144,4608]{1,0:T(8,128)} copy(f32[144,4608]{1,0:T(8,128)S(1)} %get-tuple-element.3) | data formatting | bytes 5308416

commit v4 on v3

--- a/solution.py
+++ b/solution.py
@@ -97,7 +97,6 @@
 
     load_a.wait()
     T[...] = a_ref[...].T.reshape(4, 2, HB, TB)
-    act = go(T.at[:, o], AT.at[h, :, c], ACROSS)
     AT[h, :, c] = T[:, h]
     act_own = same(AT.at[h, :, c], OTHER)
 
@@ -106,6 +105,7 @@
     l1.wait_recv()
     l2 = same(slot(h, xp, HB, HB), LEFT)
     a0.wait_recv()
+    act = go(T.at[:, o], AT.at[h, :, c], ACROSS)
     ar0 = same(slot(o, x, 0, HB), RIGHT)
     a1.wait_recv()
     al1 = same(slot(o, x, HB, HB), LEFT)

time: 101 us -> 101 us (level)
  no operation moved by 1% of the time
where the time goes in v4:
time: 101 us
  Pallas kernels  97.7 us (97%)
  local copies, waits for them, and re-layouts  2.52 us (2%)
    pallas_call x1, Pallas kernels, per_device(): pl.pallas_call(kernel, out_shape=(pltpu.VMEM((FB, TB), BF), pltpu.VMEM((H...  97.7 us
    unnamed x2, local copies, waits for them, and re-layouts  2.52 us

profile of v4, /device:TPU:9, one launch (start us, length us, event | category | flops | bytes accessed | tf_op | source)
XLA Modules:
  0.0 100.8 jit_solution(2259846973898923493)
XLA Ops:
  0.6 97.7 %shard_map.50 = (bf16[1152,512]{1,0:T(8,128)(2,1)S(1)}, f32[144,4608]{1,0:T(8,128)S(1)}) custom-call(bf16[512,1152]{1,0:T(8,128)(2,1)} %a_hbm.1, bf16[288,512]{1,0:T(8,128)(2,1)} %bitcast.3, bf16[288,18432]{1,0:T(8,128)(2,1)} %bitcast.2), custom_call_target="tpu_custom_call" | custom-call | flops 10899999744 | bytes 20000000 | tf_op jit(solution)/shard_map/pallas_call | solution.py:332
  98.3 1.0 %copy.7 = bf16[1152,512]{1,0:T(8,128)(2,1)} copy(bf16[1152,512]{1,0:T(8,128)(2,1)S(1)} %get-tuple-element.2) | data formatting | bytes 2359296
  99.3 1.5 %copy.8 = f32[144,4608]{1,0:T(8,128)} copy(f32[144,4608]{1,0:T(8,128)S(1)} %get-tuple-element.3) | data formatting | bytes 5308416
